TPU v7x, 32 devices: a whole 2x2x4 slice. The times are simulated.
32 devices in a mesh: row: 4 (over z), col: 8 (over y, x, core).
Axes of the slice: x: 2, y: 2, z: 4, core: 2. Of those that a mesh axis runs over, the one named last changes fastest.
Arguments:
- user_factors: float32 [4096, 128], P(('col', 'row')), may hold values from -16 to 16
- item_factors: bfloat16 [65536, 128], P(('row', 'col')), may hold values from -0.046875 to 0.046875
- confidence: bfloat16 [4, 8, 32768, 128], P('row', 'col'), may hold values from 0 to 40, as said below
- tile_coords: int32 [4, 8, 256, 2], P('row', 'col'), may hold values from 0 to 127, as said below
- relay_source: int32 [8, 4], P('col', 'row'), may hold values from 0 to 3, each once within a row
Outputs:
- solved: float32 [4096, 128], P(('col', 'row'))
- residual: float32 [4096, 128], P(('col', 'row'))
Inputs may be any that keep to these rules, and one draw needn't show every extreme that they name: `confidence`: zero where an entry is not observed, else between 1 and 40. `tile_coords`: within one device no (user block, item block) pair repeats; column 0 is below 4, column 1 below 128.
All inputs are finite; a program needn't handle non-finite values.
Results may differ from a plain program's by a relative error of at most 0.03.
The roundings to bfloat16 on the way count: a program that leaves them out, or rounds other values in their place, can miss the bound.
Values may be sent and summed in bfloat16 or wider, within the bound.
A program may use at most 128 MiB of HBM per device.

v0:
```python
import jax
import jax.numpy as jnp
from jax import lax
from jax.sharding import PartitionSpec as P

ITERS = 3


ridge = 0.1
epsilon = 1e-06


def conjugate(solution, combined, operate, local_part):
    residual = combined - local_part(solution)
    direction = residual
    norm_now = jnp.sum(residual * residual, axis=1, keepdims=True)
    for iteration in range(ITERS):
        image = operate(direction)
        step_size = norm_now / (jnp.sum(direction * image, axis=1, keepdims=True) + epsilon)
        solution = solution + step_size * direction
        residual = residual - step_size * image
        norm_next = jnp.sum(residual * residual, axis=1, keepdims=True)
        if iteration + 1 < ITERS:
            direction = residual + norm_next / (norm_now + epsilon) * direction
        norm_now = norm_next
    return (solution, residual)


def local(user_factors, item_factors, confidence, tile_coords, relay_source):
    tile_size = confidence.shape[-1]
    factor_width = item_factors.shape[1]
    tile_count = tile_coords.shape[2]
    coords = tile_coords[0, 0]
    weights = confidence[0, 0].reshape(tile_count, tile_size, tile_size)
    own_rows = user_factors.shape[0]
    group_rows = own_rows * lax.axis_size("row")
    group_blocks = group_rows // tile_size
    item_group = lax.all_gather(item_factors, "col", axis=0, tiled=True)
    item_tiles = item_group.reshape(-1, tile_size, factor_width)[coords[:, 1]]
    gram_matrix = lax.psum(
        jnp.dot(item_factors.T, item_factors, preferred_element_type=jnp.float32), ("row", "col")
    )
    member = (coords[:, 0][None, :] == jnp.arange(group_blocks)[:, None]).astype(jnp.float32)

    def block_sum(terms):
        summed = jnp.einsum("gt,tuk->guk", member, terms, precision=lax.Precision.HIGHEST)
        return summed.reshape(group_rows, factor_width)

    def tile_terms(direction):
        picked = direction.reshape(group_blocks, tile_size, factor_width)[coords[:, 0]]
        scores = jnp.einsum("tuk,tik->tui", picked, item_tiles, preferred_element_type=jnp.float32)
        weighted = (scores * weights).astype(jnp.bfloat16)
        return block_sum(
            jnp.einsum("tui,tik->tuk", weighted, item_tiles, preferred_element_type=jnp.float32)
        )

    targets = jnp.where(weights > 0, weights.astype(jnp.float32) + 1.0, 0.0).astype(jnp.bfloat16)
    right_side = block_sum(
        jnp.einsum("tui,tik->tuk", targets, item_tiles, preferred_element_type=jnp.float32)
    )

    def local_part(vector):
        return jnp.dot(vector, gram_matrix, precision=lax.Precision.HIGHEST) + ridge * vector

    slots = relay_source[0]

    def spread(vector):
        return lax.all_gather(vector.astype(jnp.bfloat16), "row", axis=0, tiled=True)

    def reduce_rows(partial_value):
        return lax.psum_scatter(partial_value, "row", scatter_dimension=0, tiled=True)

    def operate(vector):
        return local_part(vector) + reduce_rows(tile_terms(spread(vector)))

    combined = reduce_rows(right_side - tile_terms(spread(user_factors)))
    solution, residual = conjugate(user_factors, combined, operate, local_part)
    source_rows = (slots[:, None] * tile_size + jnp.arange(tile_size)[None, :]).reshape(-1)
    piece = lax.all_gather(solution.astype(jnp.bfloat16), "row", axis=0, tiled=True).astype(
        jnp.float32
    )
    inside = (source_rows >= 0) & (source_rows < piece.shape[0])
    taken = piece[jnp.clip(source_rows, 0, piece.shape[0] - 1)]
    solved = jnp.where(inside[:, None], taken, jnp.zeros_like(solution))
    return (solved, residual)


def solution(mesh):
    return jax.shard_map(
        local,
        mesh=mesh,
        in_specs=(
            P(("col", "row"), None),
            P(("row", "col"), None),
            P("row", "col", None, None),
            P("row", "col", None, None),
            P("col", "row"),
        ),
        out_specs=(P(("col", "row"), None), P(("col", "row"), None)),
        check_vma=False,
    )
```

profile of v0, /device:TPU:0, one launch (start us, length us, event | category | flops | bytes accessed | tf_op | source)
XLA Modules:
  0.0 453.7 jit_solution(232629263278120171)
XLA Ops:
  12.7 15.0 %all_gather.19 = bf16[512,128]{1,0:T(8,128)(2,1)S(1)} all-gather(bf16[128,128]{1,0:T(8,128)(2,1)S(1)} %convert_element_type.47), channel_id=1, replica_groups=mesh['row'=4,'col'=8] {'row'}, dimensions={0}, use_global_device_ids=true | all-gather | bytes 163840 | tf_op jit(solution)/shard_map/all_gather | solution.py:68
  50.2 10.8 %gather_fusion = bf16[256,128,128]{2,1,0:T(8,128)(2,1)} fusion(bf16[128,128,128]{2,1,0:T(8,128)(2,1)} %bitcast.119, s32[1024]{0:T(1024)S(1)} %pad_clamp_fusion.2), kind=kCustom, calls=%fused_computation | custom fusion | bytes 16778240 | tf_op jit(solution)/shard_map/gather | solution.py:39
  61.0 23.7 %fusion.38 = f32[256,128,128]{2,1,0:T(8,128)} fusion(bf16[256,128,128]{2,1,0:T(8,128)(2,1)} %gather_fusion, bf16[256,128,128]{2,1,0:T(8,128)(2,1)} %bitcast.109, bf16[256,128,128]{2,1,0:T(8,128)(2,1)} %gather_fusion.1), kind=kOutput, calls=%fused_computation.75 | convolution fusion | flops 2160066560 | bytes 41943040 | tf_op jit(solution)/shard_map/tui,tik->tuk/dot_general | solution.py:54
  84.8 15.3 %fusion.10 = f32[256,128,128]{2,1,0:T(8,128)} fusion(bf16[256,128,128]{2,1,0:T(8,128)(2,1)} %gather_fusion, pred[256,128,128]{2,1,0:T(32,128)(4,1)} %bitcast.118, bf16[256,128,128]{2,1,0:T(8,128)(2,1)} %bitcast.110), kind=kOutput, calls=%fused_computation.21 | convolution fusion | flops 1090519040 | bytes 37748736 | tf_op jit(solution)/shard_map/tui,tik->tuk/dot_general | solution.py:59
  100.1 20.6 %fusion.6 = f32[4,128,128]{2,0,1:T(4,128)S(1)} fusion(f32[256,128,128]{2,1,0:T(8,128)} %fusion.38, s32[256]{0:T(256)S(1)} %bitcast.127), kind=kOutput, calls=%fused_computation.17 | convolution fusion | flops 201327616 | bytes 17040384 | tf_op jit(solution)/shard_map/gt,tuk->guk/dot_general | solution.py:46
  120.7 15.1 %fusion.14 = f32[4,128,128]{2,0,1:T(4,128)S(1)} fusion(f32[4,128,128]{2,0,1:T(4,128)S(1)} %fusion.6, f32[256,128,128]{2,1,0:T(8,128)S(1)} %copy-done, s32[256]{0:T(256)S(1)} %bitcast.128), kind=kOutput, calls=%fused_computation.25 | convolution fusion | flops 201393152 | bytes 17302528 | tf_op jit(solution)/shard_map/gt,tuk->guk/dot_general | solution.py:46
  136.8 10.7 %all-reduce.2.cloned.1.call-done = f32[128,128]{1,0:T(8,128)} async-done(((f32[128,128]{1,0:T(8,128)}), f32[128,128]{1,0:T(8,128)}) %all-reduce.2.cloned.1.call-update) | async-done | bytes 65552 | tf_op jit(solution)/shard_map/psum | solution.py:40
  147.5 9.0 %reduce-scatter.5.cloned.1.call-done = f32[128,128]{0,1:T(8,128)} async-done(((f32[512,128]{0,1:T(8,128)}), f32[128,128]{0,1:T(8,128)}) %reduce-scatter.5.cloned.1.call-update) | async-done | bytes 65552 | tf_op jit(solution)/shard_map/reduce_scatter | solution.py:71
  157.6 12.3 %all_gather.20 = bf16[512,128]{0,1:T(8,128)(2,1)S(1)} all-gather(bf16[128,128]{0,1:T(8,128)(2,1)S(1)} %get-tuple-element.19), channel_id=1, replica_groups=mesh['row'=4,'col'=8] {'row'}, dimensions={0}, use_global_device_ids=true | all-gather | bytes 163840 | tf_op jit(solution)/shard_map/all_gather | solution.py:68
  178.5 23.7 %fusion.40 = f32[256,128,128]{2,1,0:T(8,128)} fusion(bf16[256,128,128]{2,1,0:T(8,128)(2,1)} %gather_fusion, bf16[256,128,128]{2,1,0:T(8,128)(2,1)} %bitcast.111, bf16[256,128,128]{2,1,0:T(8,128)(2,1)} %gather_fusion.2), kind=kOutput, calls=%fused_computation.77 | convolution fusion | flops 2160066560 | bytes 41943040 | tf_op jit(solution)/shard_map/tui,tik->tuk/dot_general | solution.py:54
  202.2 17.5 %copy.29 = f32[256,128,128]{1,0,2:T(8,128)} copy(f32[256,128,128]{2,1,0:T(8,128)} %fusion.40) | data formatting | bytes 33554432 | tf_op jit(solution)/shard_map/tui,tik->tuk/dot_general | solution.py:54
  219.7 8.9 %fusion.30 = f32[4,128,128]{1,0,2:T(4,128)S(1)} fusion(f32[256,128,128]{1,0,2:T(8,128)} %copy.29, s32[256]{0:T(256)S(1)} %bitcast.129), kind=kOutput, calls=%fused_computation.70 | convolution fusion | flops 201327616 | bytes 17040384 | tf_op jit(solution)/shard_map/gt,tuk->guk/dot_general | solution.py:46
  229.4 18.2 %reduce-scatter.7.cloned.1.call-done = f32[128,128]{0,1:T(8,128)} async-done(((f32[512,128]{0,1:T(8,128)}), f32[128,128]{0,1:T(8,128)}) %reduce-scatter.7.cloned.1.call-update) | async-done | bytes 65552 | tf_op jit(solution)/shard_map/reduce_scatter | solution.py:71
  248.8 12.3 %all_gather.21 = bf16[512,128]{0,1:T(8,128)(2,1)S(1)} all-gather(bf16[128,128]{0,1:T(8,128)(2,1)S(1)} %get-tuple-element.12), channel_id=1, replica_groups=mesh['row'=4,'col'=8] {'row'}, dimensions={0}, use_global_device_ids=true | all-gather | bytes 163840 | tf_op jit(solution)/shard_map/all_gather | solution.py:68
  269.9 23.7 %fusion.41 = f32[256,128,128]{2,1,0:T(8,128)} fusion(bf16[256,128,128]{2,1,0:T(8,128)(2,1)} %gather_fusion, bf16[256,128,128]{2,1,0:T(8,128)(2,1)} %bitcast.112, bf16[256,128,128]{2,1,0:T(8,128)(2,1)} %gather_fusion.3), kind=kOutput, calls=%fused_computation.78 | convolution fusion | flops 2160066560 | bytes 41943040 | tf_op jit(solution)/shard_map/tui,tik->tuk/dot_general | solution.py:54
  293.6 17.5 %copy.32 = f32[256,128,128]{1,0,2:T(8,128)} copy(f32[256,128,128]{2,1,0:T(8,128)} %fusion.41) | data formatting | bytes 33554432 | tf_op jit(solution)/shard_map/tui,tik->tuk/dot_general | solution.py:54
  311.1 8.9 %fusion.28 = f32[4,128,128]{1,0,2:T(4,128)S(1)} fusion(f32[256,128,128]{1,0,2:T(8,128)} %copy.32, s32[256]{0:T(256)S(1)} %bitcast.130), kind=kOutput, calls=%fused_computation.69 | convolution fusion | flops 201327616 | bytes 17040384 | tf_op jit(solution)/shard_map/gt,tuk->guk/dot_general | solution.py:46
  320.8 18.2 %reduce-scatter.9.cloned.1.call-done = f32[128,128]{0,1:T(8,128)} async-done(((f32[512,128]{0,1:T(8,128)}), f32[128,128]{0,1:T(8,128)}) %reduce-scatter.9.cloned.1.call-update) | async-done | bytes 65552 | tf_op jit(solution)/shard_map/reduce_scatter | solution.py:71
  340.2 12.3 %all_gather.22 = bf16[512,128]{0,1:T(8,128)(2,1)S(1)} all-gather(bf16[128,128]{0,1:T(8,128)(2,1)S(1)} %get-tuple-element.8), channel_id=1, replica_groups=mesh['row'=4,'col'=8] {'row'}, dimensions={0}, use_global_device_ids=true | all-gather | bytes 163840 | tf_op jit(solution)/shard_map/all_gather | solution.py:68
  361.3 23.7 %fusion.42 = f32[256,128,128]{2,1,0:T(8,128)} fusion(bf16[256,128,128]{2,1,0:T(8,128)(2,1)} %gather_fusion, bf16[256,128,128]{2,1,0:T(8,128)(2,1)} %bitcast.113, bf16[256,128,128]{2,1,0:T(8,128)(2,1)} %gather_fusion.4), kind=kOutput, calls=%fused_computation.79 | convolution fusion | flops 2160066560 | bytes 41943040 | tf_op jit(solution)/shard_map/tui,tik->tuk/dot_general | solution.py:54
  385.0 17.5 %copy.35 = f32[256,128,128]{1,0,2:T(8,128)} copy(f32[256,128,128]{2,1,0:T(8,128)} %fusion.42) | data formatting | bytes 33554432 | tf_op jit(solution)/shard_map/tui,tik->tuk/dot_general | solution.py:54
  402.5 8.9 %fusion.26 = f32[4,128,128]{1,0,2:T(4,128)S(1)} fusion(f32[256,128,128]{1,0,2:T(8,128)} %copy.35, s32[256]{0:T(256)S(1)} %bitcast.131), kind=kOutput, calls=%fused_computation.68 | convolution fusion | flops 201327616 | bytes 17040384 | tf_op jit(solution)/shard_map/gt,tuk->guk/dot_general | solution.py:46
  412.8 17.7 %reduce-scatter.11.cloned.1.call-done = f32[128,128]{0,1:T(8,128)} async-done(((f32[512,128]{0,1:T(8,128)}), f32[128,128]{0,1:T(8,128)}) %reduce-scatter.11.cloned.1.call-update) | async-done | bytes 65552 | tf_op jit(solution)/shard_map/reduce_scatter | solution.py:71
  431.7 12.3 %all_gather.23 = bf16[512,128]{0,1:T(8,128)(2,1)S(1)} all-gather(bf16[128,128]{0,1:T(8,128)(2,1)S(1)} %get-tuple-element.18), channel_id=1, replica_groups=mesh['row'=4,'col'=8] {'row'}, dimensions={0}, use_global_device_ids=true | all-gather | bytes 163840 | tf_op jit(solution)/shard_map/all_gather | solution.py:79
  (59 shorter events, 63.8 us)
Async XLA Ops:
  8.0 42.2 %all-gather.2.cloned.1.call-start = ((), (), s32[]{:S(2)}) async-start(), calls=%async_computation.4 | async-start | bytes 4718592 | tf_op jit(solution)/shard_map/all_gather | solution.py:38
  8.7 138.8 %all-reduce.2.cloned.1.call-start = ((), (), s32[]{:S(2)}) async-start(), calls=%async_computation.6 | async-start | bytes 131072 | tf_op jit(solution)/shard_map/psum | solution.py:40
  11.0 145.5 %reduce-scatter.5.cloned.1.call-start = ((), (), s32[]{:S(2)}) async-start(), calls=%async_computation.5 | async-start | bytes 327680 | tf_op jit(solution)/shard_map/reduce_scatter | solution.py:71
  100.1 20.6 %copy-start = (f32[256,128,128]{2,1,0:T(8,128)S(1)}, f32[256,128,128]{2,1,0:T(8,128)}, u32[]{:S(2)}) copy-start(f32[256,128,128]{2,1,0:T(8,128)} %fusion.10) | copy-start | bytes 50331652
  120.7 16.0 %copy-start.2 = (f32[128,128]{1,0:T(8,128)S(1)}, f32[128,128]{1,0:T(8,128)}, u32[]{:S(2)}) copy-start(f32[128,128]{1,0:T(8,128)} %param.5) | copy-start | bytes 196612
  136.7 110.9 %reduce-scatter.7.cloned.1.call-start = ((), (), s32[]{:S(2)}) async-start(), calls=%async_computation.7 | async-start | bytes 327680 | tf_op jit(solution)/shard_map/reduce_scatter | solution.py:71
  219.7 27.9 %copy-start.1 = (f32[128,128]{1,0:T(8,128)S(1)}, f32[128,128]{1,0:T(8,128)}, u32[]{:S(2)}) copy-start(f32[128,128]{1,0:T(8,128)} %all-reduce.2.cloned.1.call-done) | copy-start | bytes 196612
  229.3 109.6 %reduce-scatter.9.cloned.1.call-start = ((), (), s32[]{:S(2)}) async-start(), calls=%async_computation.8 | async-start | bytes 327680 | tf_op jit(solution)/shard_map/reduce_scatter | solution.py:71
  320.7 109.8 %reduce-scatter.11.cloned.1.call-start = ((), (), s32[]{:S(2)}) async-start(), calls=%async_computation.9 | async-start | bytes 327680 | tf_op jit(solution)/shard_map/reduce_scatter | solution.py:71
Sparse Core Ops, SparseCore 0:
  10.7 39.4 all-gather.1
  136.8 19.6 reduce-scatter.4
  229.4 18.1 reduce-scatter.6
  320.8 18.0 reduce-scatter.8
  412.2 18.2 reduce-scatter.10
Sparse Core Ops, SparseCore 1:
  16.3 131.1 all-reduce.1
where the time goes:
time: 463 us; the launch traced here: 454 us
  matrix products  179 us (39%)
  local copies, waits for them, and re-layouts  103 us (22%)
  waiting for transfers between devices  81.8 us (18%)
  blocking collectives  64.1 us (14%)
  between operations  16.5 us (4%)
  other arithmetic  9.25 us (2%)
    dot_general x4, matrix products, tile_terms(): jnp.einsum('tui,tik->tuk', weighted, item_tiles, preferred_element_type=j...  94.8 us
    reduce_scatter x4, waiting for transfers between devices, reduce_rows(): lax.psum_scatter(partial_value, 'row', scatter_dimension=0, tiled=True)  63 us
    dot_general x5, matrix products, block_sum(): jnp.einsum('gt,tuk->guk', member, terms, precision=lax.Precision.HIGHEST)  62.3 us
    dot_general x3, local copies, waits for them, and re-layouts, tile_terms(): jnp.einsum('tui,tik->tuk', weighted, item_tiles, preferred_element_type=j...  52.4 us
    all_gather x4, blocking collectives, spread(): lax.all_gather(vector.astype(jnp.bfloat16), 'row', axis=0, tiled=True)  51.8 us
    gather x4, local copies, waits for them, and re-layouts, tile_terms(): direction.reshape(group_blocks, tile_size, factor_width)[coords[:, 0]]  34.5 us
    dot_general x1, matrix products, local(): jnp.einsum('tui,tik->tuk', targets, item_tiles, preferred_element_type=jn...  15.3 us
    all_gather x1, blocking collectives, local(): lax.all_gather(solution.astype(jnp.bfloat16), 'row', axis=0, tiled=True)  12.3 us
  transfers between devices with their start and end apart: 6, of which 6 were waited for; matrix products, arithmetic and copies ran while one was open for 23% of the time, Pallas kernels for 0%

commit v1 on v0

v1 whole, which is shorter than its diff:
```python
import functools

import jax
import jax.numpy as jnp
from jax import lax
from jax.experimental import pallas as pl
from jax.experimental.pallas import tpu as pltpu
from jax.sharding import PartitionSpec as P

ITERS = 3
RIDGE = 0.1
EPSILON = 1e-06
HALVES = 2
WIDE = 4


def flip(index, mask):
    bit = 1
    while bit <= mask:
        if mask & bit:
            index = index + bit * (1 - 2 * ((index // bit) % 2))
        bit *= 2
    return index


def route(offset, half):
    if offset % 2:
        return 1
    bits = [1 << i for i in range(offset.bit_length()) if offset >> i & 1]
    if len(bits) == 2:
        return bits[1 - half]
    return offset


def kernel(
    n_row, n_col, size,
    where_ref, slot_ref, user_ref, item_ref, conf_ref,
    solved_ref, resid_ref,
    weights, items, start_users, users, part, inbox, gram, gram_in, steps, direction,
    conf_sem, item_sem, gather_send, gather_recv, row_send, row_recv,
):
    row = lax.axis_index("row")
    col = lax.axis_index("col")
    shard = item_ref.shape[0]
    half_rows = shard // HALVES
    item_blocks = items.shape[0] // size
    own_blocks = shard // size
    user_blocks = n_row
    own = pl.ds(pl.multiple_of(row * size, size), size)

    def shard_rows(mask, half):
        start = flip(col, mask) * shard + half * half_rows
        return pl.ds(pl.multiple_of(start, size), half_rows)

    def gather_copy(offset, half):
        delta = route(offset, half)
        held = delta ^ offset
        there = shard_rows(held, half)
        source = items.at[there] if held else item_ref.at[pl.ds(half * half_rows, half_rows)]
        return pltpu.make_async_remote_copy(
            src_ref=source,
            dst_ref=items.at[there],
            send_sem=gather_send.at[offset, half],
            recv_sem=gather_recv.at[offset, half],
            device_id=(row, flip(col, delta)),
            device_id_type=pl.DeviceIdType.MESH,
        )

    def peer(d):
        return (row + d) % n_row

    def row_copy(kind, d, source, target):
        return pltpu.make_async_remote_copy(
            src_ref=source,
            dst_ref=target,
            send_sem=row_send.at[kind, d],
            recv_sem=row_recv.at[kind, d],
            device_id=(peer(d), col),
            device_id_type=pl.DeviceIdType.MESH,
        )

    def start_copy(d):
        return row_copy(0, d, user_ref, start_users.at[row])

    def gram_copy(d):
        return row_copy(1, d, gram, gram_in.at[d - 1])

    def sum_copy(phase, d):
        block = pl.ds(pl.multiple_of(peer(d) * size, size), size)
        return row_copy(2 + phase, d, part.at[phase, block], inbox.at[phase, d - 1])

    def users_copy(step, d):
        return row_copy(3 + ITERS + step, d, users.at[step + 1, row], users.at[step + 1, row])

    def steps_copy(step, d):
        return row_copy(3 + 2 * ITERS + step, d, steps.at[step, row], steps.at[step, row])

    peers = range(1, n_row)
    loaded = pltpu.make_async_copy(conf_ref, weights.at[pl.ds(0, conf_ref.shape[0])], conf_sem)
    loaded.start()
    own_items = pltpu.make_async_copy(
        item_ref, items.at[pl.ds(pl.multiple_of(col * shard, size), shard)], item_sem
    )
    own_items.start()

    deltas = sorted({route(m, h) for m in range(1, n_col) for h in range(HALVES)})
    barrier = pltpu.get_barrier_semaphore()
    for d in peers:
        pl.semaphore_signal(
            barrier, inc=1, device_id=(peer(d), col), device_id_type=pl.DeviceIdType.MESH
        )
    for delta in deltas:
        pl.semaphore_signal(
            barrier, inc=1, device_id=(row, flip(col, delta)), device_id_type=pl.DeviceIdType.MESH
        )
    pl.semaphore_wait(barrier, n_row - 1 + len(deltas))

    pending = [(m, h) for m in range(1, n_col) for h in range(HALVES)]
    begun = []
    arrived = set()

    def send_ready(offset, half):
        for m, h in pending:
            if h == half and (route(m, h) ^ m) == offset and (m, h) not in begun:
                gather_copy(m, h).start()
                begun.append((m, h))

    def receive(offset, half):
        if (offset, half) not in arrived:
            gather_copy(offset, half).wait_recv()
            arrived.add((offset, half))
            send_ready(offset, half)

    for d in peers:
        start_copy(d).start()
    direct = [m for m in range(1, n_col) if all(route(m, h) == m for h in range(HALVES))]
    singles = [m for m in direct if m != 1]
    for turn in range(HALVES):
        for place, m in enumerate(singles):
            half = (turn + place) % HALVES
            gather_copy(m, half).start()
            begun.append((m, half))
        if turn == 0:
            for half in range(HALVES):
                gather_copy(1, half).start()
                begun.append((1, half))

    weights[conf_ref.shape[0]] = jnp.zeros((size, size), weights.dtype)
    start_users[row] = user_ref[...]
    part[...] = jnp.zeros_like(part)
    gram[...] = jnp.zeros_like(gram)
    loaded.wait()
    own_items.wait()
    for d in peers:
        start_copy(d).wait_recv()
    users[0] = start_users[...].astype(jnp.bfloat16)

    def weight_tile(block, item_block):
        tile = where_ref[block * item_blocks + item_block]
        return weights[tile]

    def terms(phase, first_block):
        rows = pl.ds(pl.multiple_of(first_block * size, size), WIDE * size)
        factors = items[rows, :]
        for block in range(user_blocks):
            mine = pl.ds(block * size, size)
            scores = lax.dot_general(
                users[phase, block], factors, (((1,), (1,)), ((), ())),
                preferred_element_type=jnp.float32,
            )
            w = jnp.concatenate(
                [weight_tile(block, first_block + i) for i in range(WIDE)], axis=1
            ).astype(jnp.float32)
            weighted = (scores * w).astype(jnp.bfloat16)
            total = jnp.dot(weighted, factors, preferred_element_type=jnp.float32)
            if phase == 0:
                targets = jnp.where(w > 0, w + 1.0, 0.0).astype(jnp.bfloat16)
                total = jnp.dot(targets, factors, preferred_element_type=jnp.float32) - total
            part[phase, mine, :] += total
        if phase == 0:
            gram[...] += lax.dot_general(
                factors, factors, (((0,), (0,)), ((), ())), preferred_element_type=jnp.float32
            )

    def first_pass(offset):
        base = flip(col, offset) * own_blocks

        def body(i, carry):
            terms(0, base + i * WIDE)
            return carry

        lax.fori_loop(0, own_blocks // WIDE, body, 0)

    evens = [m for m in range(2, n_col, 2)]
    early = [m for m in evens if m in singles]
    late = [m for m in evens if m not in singles]
    first_pass(0)
    for place, m in enumerate(early):
        receive(m, place % HALVES)
    for half in range(HALVES):
        receive(1, half)
    first_pass(1)
    for place, m in enumerate(early):
        receive(m, (place + 1) % HALVES)
    for m in early:
        first_pass(m)
    for m in late:
        for half in range(HALVES):
            receive(m, half)
    for m in early:
        for half in range(HALVES):
            receive(m + 1, half)
        first_pass(m + 1)
    for m in late:
        first_pass(m)
    for m in late:
        for half in range(HALVES):
            receive(m + 1, half)
        first_pass(m + 1)

    part[0] -= jnp.dot(
        start_users[...].reshape(part.shape[1:]), gram[...], precision=lax.Precision.HIGHEST,
        preferred_element_type=jnp.float32,
    )
    for d in peers:
        sum_copy(0, d).start()
    for d in peers:
        gram_copy(d).start()
    residual = part[0, own, :] - RIDGE * user_ref[...]
    for d in peers:
        sum_copy(0, d).wait_recv()
    for d in peers:
        residual += inbox[0, d - 1]
    resid_ref[...] = residual
    direction[...] = residual
    norm_now = jnp.sum(residual * residual, axis=1, keepdims=True)

    for step in range(ITERS):
        users[step + 1, row] = direction[...].astype(jnp.bfloat16)
        for d in peers:
            users_copy(step, d).start()
        for d in peers:
            users_copy(step, d).wait_recv()

        def body(i, carry, phase=step + 1):
            terms(phase, i * WIDE)
            return carry

        lax.fori_loop(0, item_blocks // WIDE, body, 0)
        for d in peers:
            sum_copy(step + 1, d).start()
        if step == 0:
            for d in peers:
                gram_copy(d).wait()
            whole = gram[...]
            for d in peers:
                whole += gram_in[d - 1]
            gram[...] = whole
        vector = direction[...]
        image = (
            jnp.dot(
                vector, gram[...], precision=lax.Precision.HIGHEST,
                preferred_element_type=jnp.float32,
            )
            + RIDGE * vector
            + part[step + 1, own, :]
        )
        for d in peers:
            sum_copy(step + 1, d).wait_recv()
        for d in peers:
            image += inbox[step + 1, d - 1]
        step_size = norm_now / (jnp.sum(vector * image, axis=1, keepdims=True) + EPSILON)
        spread = jnp.broadcast_to(step_size, (size, size))
        steps[step, row] = spread.T[:8]
        for d in peers:
            steps_copy(step, d).start()
        residual = resid_ref[...] - step_size * image
        resid_ref[...] = residual
        norm_next = jnp.sum(residual * residual, axis=1, keepdims=True)
        direction[...] = residual + norm_next / (norm_now + EPSILON) * vector
        norm_now = norm_next

    for step in range(ITERS):
        for d in peers:
            steps_copy(step, d).wait_recv()
    source = slot_ref[0, 0]
    answer = start_users[source]
    for step in range(ITERS):
        scale = jnp.broadcast_to(steps[step, source][0:1], (size, size)).T
        answer += scale * users[step + 1, source].astype(jnp.float32)
    solved_ref[...] = answer

    for m, h in pending:
        gather_copy(m, h).wait_send()
    for d in peers:
        start_copy(d).wait_send()
        for phase in range(ITERS + 1):
            sum_copy(phase, d).wait_send()
        for step in range(ITERS):
            users_copy(step, d).wait_send()
            steps_copy(step, d).wait_send()


def local(n_row, n_col, user_factors, item_factors, confidence, tile_coords, relay_source):
    size = confidence.shape[-1]
    width = item_factors.shape[1]
    tiles = tile_coords.shape[2]
    group_items = item_factors.shape[0] * n_col
    item_blocks = group_items // size
    group_users = user_factors.shape[0] * n_row
    coords = tile_coords[0, 0]
    key = coords[:, 0] * item_blocks + coords[:, 1]
    places = jnp.arange(n_row * item_blocks, dtype=jnp.int32)
    number = jnp.arange(tiles, dtype=jnp.int32)
    where = jnp.min(
        jnp.where(key[None, :] == places[:, None], number[None, :], tiles), axis=1
    ).astype(jnp.int32)
    kinds = 3 + 3 * ITERS
    vmem = pl.BlockSpec(memory_space=pltpu.VMEM)
    smem = pl.BlockSpec(memory_space=pltpu.SMEM)
    outs = jax.ShapeDtypeStruct(user_factors.shape, jnp.float32)
    return pl.pallas_call(
        functools.partial(kernel, n_row, n_col, size),
        out_shape=(outs, outs),
        in_specs=[smem, smem, vmem, vmem, pl.BlockSpec(memory_space=pl.ANY)],
        out_specs=(vmem, vmem),
        scratch_shapes=[
            pltpu.VMEM((tiles + 1, size, size), jnp.bfloat16),
            pltpu.VMEM((group_items, width), jnp.bfloat16),
            pltpu.VMEM((n_row, size, width), jnp.float32),
            pltpu.VMEM((ITERS + 1, n_row, size, width), jnp.bfloat16),
            pltpu.VMEM((ITERS + 1, group_users, width), jnp.float32),
            pltpu.VMEM((ITERS + 1, n_row - 1, size, width), jnp.float32),
            pltpu.VMEM((width, width), jnp.float32),
            pltpu.VMEM((n_row - 1, width, width), jnp.float32),
            pltpu.VMEM((ITERS, n_row, 8, size), jnp.float32),
            pltpu.VMEM((size, width), jnp.float32),
            pltpu.SemaphoreType.DMA,
            pltpu.SemaphoreType.DMA,
            pltpu.SemaphoreType.DMA((n_col, HALVES)),
            pltpu.SemaphoreType.DMA((n_col, HALVES)),
            pltpu.SemaphoreType.DMA((kinds, n_row)),
            pltpu.SemaphoreType.DMA((kinds, n_row)),
        ],
        compiler_params=pltpu.CompilerParams(
            collective_id=0, has_side_effects=True, vmem_limit_bytes=48 * 2**20
        ),
    )(where, relay_source, user_factors, item_factors, confidence.reshape(tiles, size, size))


def solution(mesh):
    return jax.shard_map(
        functools.partial(local, mesh.shape["row"], mesh.shape["col"]),
        mesh=mesh,
        in_specs=(
            P(("col", "row"), None),
            P(("row", "col"), None),
            P("row", "col", None, None),
            P("row", "col", None, None),
            P("col", "row"),
        ),
        out_specs=(P(("col", "row"), None), P(("col", "row"), None)),
        check_vma=False,
    )
```

time: 463 us -> 178 us (0.38); the launches traced: 454 us -> 177 us
  matrix products: 179 us -> 0 us
  Pallas kernels: 0 us -> 172 us
  local copies, waits for them, and re-layouts: 103 us -> 3.14 us
  waiting for transfers between devices: 81.8 us -> 0 us
  blocking collectives: 64.1 us -> 0 us
  between operations: 16.5 us -> 1.3 us
  other arithmetic: 9.25 us -> 0.91 us
    dot_general x15 -> x0, matrix products: 179 us -> none  [the longest x4 94.8 us: tile_terms(): jnp.einsum('tui,tik->tuk', weighted, item_tiles, preferred_element_type=j...]
    pallas_call x0 -> x1, Pallas kernels: none -> 172 us  [local(): pl.pallas_call(functools.partial(kernel, n_row, n_col, size), out_shape=(...]
    all_gather x5 -> x0, blocking collectives: 64.1 us -> none  [the longest x4 51.8 us: spread(): lax.all_gather(vector.astype(jnp.bfloat16), 'row', axis=0, tiled=True)]
    reduce_scatter x4 -> x0, waiting for transfers between devices: 63 us -> none  [reduce_rows(): lax.psum_scatter(partial_value, 'row', scatter_dimension=0, tiled=True)]
    dot_general x3 -> x0, local copies, waits for them, and re-layouts: 52.4 us -> none  [tile_terms(): jnp.einsum('tui,tik->tuk', weighted, item_tiles, preferred_element_type=j...]
    gather x6 -> x0, local copies, waits for them, and re-layouts: 46 us -> none  [the longest x4 34.5 us: tile_terms(): direction.reshape(group_blocks, tile_size, factor_width)[coords[:, 0]]]
    psum x1 -> x0, waiting for transfers between devices: 10.7 us -> none  [local(): lax.psum(jnp.dot(item_factors.T, item_factors, preferred_element_type=jnp...]
    all_gather x1 -> x0, waiting for transfers between devices: 7.33 us -> none  [local(): item_group = lax.all_gather(item_factors, 'col', axis=0, tiled=True)]
  transfers between devices with their start and end apart: 6 -> 0, of which waited for: 6 -> 0; matrix products, arithmetic and copies ran while one was open for 23% -> 0% of each run, Pallas kernels for 0% -> 0%
where the time goes in v1:
time: 178 us; the launch traced here: 177 us
  Pallas kernels  172 us (97%)
  local copies, waits for them, and re-layouts  3.14 us (2%)
    pallas_call x1, Pallas kernels, local(): pl.pallas_call(functools.partial(kernel, n_row, n_col, size), out_shape=(...  172 us

profile of v1, /device:TPU:0, one launch (start us, length us, event | category | flops | bytes accessed | tf_op | source)
XLA Modules:
  0.0 177.5 jit_solution(16184278012269796125)
XLA Ops:
  1.3 0.8 slice_add_fusion
  2.0 0.1 select_reduce_fusion.where_ref
  2.2 0.0 copy-start
  2.2 1.0 copy-done
  3.2 0.0 copy-start.1
  3.2 0.8 copy-done.1
  4.1 172.2 %shard_map.68 = (f32[128,128]{1,0:T(8,128)S(1)}, f32[128,128]{1,0:T(8,128)S(1)}) custom-call(s32[512]{0:T(512)S(1)} %select_reduce_fusion.where_ref, s32[1,1]{1,0:T(1,128)S(6)} %copy.9.slot_ref, f32[128,128]{1,0:T(8,128)S(1)} %copy-done.1, bf16[2048,128]{1,0:T(8,128)(2,1)S(1)} %copy-done, bf16[256,128,128]{2,1,0:T(8,128)(2,1)} %bitcast.3), custom_call_target="tpu_custom_call" | custom-call | tf_op jit(solution)/shard_map/pallas_call | solution.py:322
  176.2 0.6 copy.10
  176.9 0.6 copy.11
Async XLA Ops:
  2.2 1.0 copy-start
  3.2 0.8 copy-start.1

commit v2 on v1

--- a/solution.py
+++ b/solution.py
@@ -162,21 +162,25 @@
     def terms(phase, first_block):
         rows = pl.ds(pl.multiple_of(first_block * size, size), WIDE * size)
         factors = items[rows, :]
-        for block in range(user_blocks):
-            mine = pl.ds(block * size, size)
-            scores = lax.dot_general(
-                users[phase, block], factors, (((1,), (1,)), ((), ())),
-                preferred_element_type=jnp.float32,
-            )
-            w = jnp.concatenate(
-                [weight_tile(block, first_block + i) for i in range(WIDE)], axis=1
-            ).astype(jnp.float32)
-            weighted = (scores * w).astype(jnp.bfloat16)
-            total = jnp.dot(weighted, factors, preferred_element_type=jnp.float32)
-            if phase == 0:
-                targets = jnp.where(w > 0, w + 1.0, 0.0).astype(jnp.bfloat16)
-                total = jnp.dot(targets, factors, preferred_element_type=jnp.float32) - total
-            part[phase, mine, :] += total
+        scores = lax.dot_general(
+            users[phase].reshape(part.shape[1:]), factors, (((1,), (1,)), ((), ())),
+            preferred_element_type=jnp.float32,
+        )
+        w = jnp.concatenate(
+            [
+                jnp.concatenate(
+                    [weight_tile(block, first_block + i) for i in range(WIDE)], axis=1
+                )
+                for block in range(user_blocks)
+            ],
+            axis=0,
+        ).astype(jnp.float32)
+        weighted = (scores * w).astype(jnp.bfloat16)
+        total = jnp.dot(weighted, factors, preferred_element_type=jnp.float32)
+        if phase == 0:
+            targets = jnp.where(w > 0, w + 1.0, 0.0).astype(jnp.bfloat16)
+            total = jnp.dot(targets, factors, preferred_element_type=jnp.float32) - total
+        part[phase] += total
         if phase == 0:
             gram[...] += lax.dot_general(
                 factors, factors, (((0,), (0,)), ((), ())), preferred_element_type=jnp.float32

time: 178 us -> 131 us (0.74)
  Pallas kernels: 172 us -> 125 us
    pallas_call x1, Pallas kernels: 172 us -> 125 us  [local(): pl.pallas_call(functools.partial(kernel, n_row, n_col, size), out_shape=(...]
where the time goes in v2:
time: 131 us
  Pallas kernels  125 us (95%)
  local copies, waits for them, and re-layouts  3.14 us (2%)
    pallas_call x1, Pallas kernels, local(): pl.pallas_call(functools.partial(kernel, n_row, n_col, size), out_shape=(...  125 us
    unnamed x6, local copies, waits for them, and re-layouts  3.14 us

profile of v2, /device:TPU:0, one launch (start us, length us, event | category | flops | bytes accessed | tf_op | source)
XLA Modules:
  0.0 130.6 jit_solution(472252372330667823)
XLA Ops:
  1.3 0.8 slice_add_fusion
  2.0 0.1 select_reduce_fusion.where_ref
  2.2 0.0 copy-start
  2.2 1.0 copy-done
  3.2 0.0 copy-start.1
  3.2 0.8 copy-done.1
  4.1 125.3 %shard_map.68 = (f32[128,128]{1,0:T(8,128)S(1)}, f32[128,128]{1,0:T(8,128)S(1)}) custom-call(s32[512]{0:T(512)S(1)} %select_reduce_fusion.where_ref, s32[1,1]{1,0:T(1,128)S(6)} %copy.9.slot_ref, f32[128,128]{1,0:T(8,128)S(1)} %copy-done.1, bf16[2048,128]{1,0:T(8,128)(2,1)S(1)} %copy-done, bf16[256,128,128]{2,1,0:T(8,128)(2,1)} %bitcast.3), custom_call_target="tpu_custom_call" | custom-call | tf_op jit(solution)/shard_map/pallas_call | solution.py:326
  129.3 0.6 copy.10
  130.0 0.6 copy.11
Async XLA Ops:
  2.2 1.0 copy-start
  3.2 0.8 copy-start.1
